TPU v7x, 256 devices: a whole 4x4x8 slice. The times are simulated.
256 devices in a mesh: sec: 2 (over y_hi), dp: 16 (over y_lo, x, core), mp: 8 (over z).
Axes of the slice: x: 4, y: 4 (y_hi: 2, y_lo: 2; y = y_hi * 2 + y_lo), z: 8, core: 2. Of those that a mesh axis runs over, the one named last changes fastest.
Arguments:
- hidden_pre: bfloat16 [16384, 12288], P('dp', 'mp'), may hold values from -6 to 6
- residual: bfloat16 [16384, 3072], P('dp', 'mp'), may hold values from -64 to 64
- w_down: bfloat16 [3072, 12288], P('dp', 'mp'), may hold values from -0.0546875 to 0.0546875
- head_weight: bfloat16 [3072, 4096], P('dp', 'mp'), may hold values from -0.109375 to 0.109375
- norm_gain: float32 [3072], replicated, may hold values from 0.5 to 1.5
- segment_logits: bfloat16 [2, 16384, 4096], P('sec', ('dp', 'mp')), may hold values from -64 to 320
- student_hidden: bfloat16 [16384, 1024], P(('dp', 'mp')), may hold values from -24 to 24
- frame_mask: int32 [16384], P(('dp', 'mp')), may hold values 0 or 1
Outputs:
- segment_out: bfloat16 [2, 16384, 4096], P('sec', ('dp', 'mp'))
- grad_out: float32 [2, 1024, 4096], P('sec', ('dp', 'mp'))
All inputs are finite; a program needn't handle non-finite values. No bound on the sum of `frame_mask` on one device may be relied on, other than what follows from the above.
Results may differ from a plain program's by a relative error of at most 0.015.
Values may be sent and summed in bfloat16 or wider, within the bound.
No kernel may reach another device: no remote copies, remote signals or barrier semaphores. Data moves between devices by JAX's collectives and lax.ppermute only.
A program may use at most 128 MiB of HBM per device.

v0:
```python
import jax
import jax.numpy as jnp
from jax import lax
from jax.sharding import PartitionSpec as P


def passed_along(block, axis, distance):
    devices = range(lax.axis_size(axis))
    route = [(i - distance, i) for i in devices if i - distance in devices]
    return lax.ppermute(block, axis, route)


def teacher_work(hidden_pre, residual, w_down, head_weight, norm_gain):
    active = jax.nn.silu(hidden_pre.astype(jnp.float32)).astype(jnp.bfloat16)
    partial_sum = lax.dot_general(
        active,
        lax.all_gather(w_down, "dp", axis=0, tiled=True),
        (((1,), (1,)), ((), ())),
        preferred_element_type=jnp.float32,
    )
    down_sum = lax.psum(partial_sum.astype(jnp.bfloat16), "mp").astype(jnp.float32)
    whole = lax.all_gather(residual, "mp", axis=1, tiled=True)
    middle = whole.astype(jnp.float32) + 0.5 * down_sum
    center = jnp.mean(middle, axis=1, keepdims=True)
    spread = jnp.mean(middle * middle, axis=1, keepdims=True) - center * center
    normed = ((middle - center) * lax.rsqrt(spread + 1e-05) * norm_gain).astype(jnp.bfloat16)
    logits = jnp.dot(
        normed,
        lax.all_gather(head_weight, "dp", axis=0, tiled=True),
        preferred_element_type=jnp.float32,
    )
    return lax.all_to_all(
        logits.astype(jnp.bfloat16), "mp", split_axis=0, concat_axis=1, tiled=True
    )


def student_work(received, own_logits, student_hidden, frame_mask):
    teacher_post = jax.nn.softmax(received.astype(jnp.float32), axis=-1)
    student_post = jax.nn.softmax(own_logits.astype(jnp.float32), axis=-1)
    weights = frame_mask.astype(jnp.float32)[:, None]
    logit_grad = (weights * (student_post - teacher_post)).astype(jnp.bfloat16)
    summed = lax.psum_scatter(
        lax.dot_general(
            student_hidden, logit_grad, (((0,), (0,)), ((), ())), preferred_element_type=jnp.float32
        ),
        ("dp", "mp"),
        scatter_dimension=0,
        tiled=True,
    )
    return (logit_grad, summed)


def body(
    hidden_pre, residual, w_down, head_weight, norm_gain, segment_logits, student_hidden, frame_mask
):
    received = passed_along(segment_logits[0], "sec", 1)
    regrouped = teacher_work(hidden_pre, residual, w_down, head_weight, norm_gain)
    logit_grad, summed = student_work(received, segment_logits[0], student_hidden, frame_mask)
    is_teacher = lax.axis_index("sec") == 0
    segment_piece = jnp.where(is_teacher, regrouped, logit_grad)
    grad_piece = jnp.where(is_teacher, jnp.zeros_like(summed), summed)
    return (segment_piece[None], grad_piece[None])


def solution(mesh):
    placed = (
        P("dp", "mp"),
        P("dp", "mp"),
        P("dp", "mp"),
        P("dp", "mp"),
        P(),
        P("sec", ("dp", "mp"), None),
        P(("dp", "mp"), None),
        P(("dp", "mp")),
    )
    return jax.shard_map(
        body,
        mesh=mesh,
        in_specs=placed,
        out_specs=(P("sec", ("dp", "mp"), None), P("sec", ("dp", "mp"), None)),
        check_vma=False,
    )
```

profile of v0, /device:TPU:0, one launch (start us, length us, event | category | flops | bytes accessed | tf_op | source)
XLA Modules:
  0.0 836.3 jit_solution(2691578813722732034)
XLA Ops:
  8.1 0.7 all-gather.6.cloned.1.call-update
  8.8 0.7 all-gather.4.cloned.1.call-update
  9.5 62.0 %all-gather.6.cloned.1.call-done = bf16[3072,1536]{1,0:T(8,128)(2,1)} async-done(((bf16[192,1536]{1,0:T(8,128)(2,1)}), bf16[3072,1536]{1,0:T(8,128)(2,1)}) %all-gather.6.cloned.1.call-update) | async-done | bytes 9437200 | tf_op jit(solution)/shard_map/all_gather | solution.py:17
  71.6 15.2 %convolution_convert_fusion = bf16[1024,3072]{1,0:T(8,128)(2,1)} fusion(bf16[3072,1536]{1,0:T(8,128)(2,1)} %all-gather.6.cloned.1.call-done, bf16[1024,1536]{1,0:T(8,128)(2,1)} %param.8), kind=kOutput, calls=%fused_computation.12 | convolution fusion | flops 9676259328 | bytes 18874368 | tf_op jit(solution)/shard_map/dot_general | solution.py:15
  86.8 0.5 all-gather.8.cloned.1.call-update
  87.4 0.6 copy-done.2
  87.9 5.0 collective-permute-start
  93.3 0.5 fusion.9
  93.8 21.8 %collective-permute-done = bf16[128,4096]{1,0:T(8,128)(2,1)S(1)} collective-permute-done((bf16[128,4096]{1,0:T(8,128)(2,1)S(1)}, bf16[128,4096]{1,0:T(8,128)(2,1)S(1)}, u32[]{:S(2)}, u32[]{:S(2)}) %collective-permute-start) | collective-permute-done | bytes 1048608 | tf_op jit(solution)/shard_map/ppermute | solution.py:10
  115.8 0.5 fusion.8
  116.3 8.6 %convolution_bitcast_fusion = f32[1024,4096]{0,1:T(8,128)} fusion(bf16[128,1024]{1,0:T(8,128)(2,1)S(1)} %copy-done, bf16[128,4096]{1,0:T(8,128)(2,1)S(1)} %collective-permute-done, f32[128]{0:T(128)S(1)} %fusion.8, f32[128]{0:T(128)S(1)} %reduce_max.31, f32[128]{0:T(128)S(1)} %fusion.9, f32[128]{0:T(128)S(1)} %reduce_max.29, ...), kind=kOutput, calls=%fused_computation.4 | convolution fusion | flops 1078460416 | bytes 19139072 | tf_op jit(solution)/shard_map/dot_general | solution.py:43
  124.9 17.6 %copy.14 = f32[1024,4096]{1,0:T(8,128)} copy(f32[1024,4096]{0,1:T(8,128)} %convolution_bitcast_fusion) | data formatting | bytes 33554432
  142.5 6.3 all-gather.4.cloned.1.call-done
  148.8 166.1 %all-reduce.2.cloned.1.call-done = bf16[1024,3072]{1,0:T(8,128)(2,1)} async-done(((bf16[1024,3072]{1,0:T(8,128)(2,1)}), bf16[1024,3072]{1,0:T(8,128)(2,1)}) %all-reduce.2.cloned.1.call-update) | async-done | bytes 6291472 | tf_op jit(solution)/shard_map/psum | solution.py:21
  314.9 6.6 fusion
  321.6 34.6 %all-gather.8.cloned.1.call-done = bf16[3072,512]{1,0:T(8,128)(2,1)} async-done(((bf16[192,512]{1,0:T(8,128)(2,1)}), bf16[3072,512]{1,0:T(8,128)(2,1)}) %all-gather.8.cloned.1.call-update) | async-done | bytes 3145744 | tf_op jit(solution)/shard_map/all_gather | solution.py:29
  356.2 10.0 %fusion.10 = bf16[1024,512]{1,0:T(8,128)(2,1)} fusion(bf16[3072,512]{1,0:T(8,128)(2,1)} %all-gather.8.cloned.1.call-done, bf16[1024,3072]{1,0:T(8,128)(2,1)} %all-reduce.2.cloned.1.call-done, bf16[1024,3072]{1,0:T(8,128)(2,1)} %all-gather.4.cloned.1.call-done, f32[3072]{0:T(1024)S(1)} %copy-done.3, f32[1024]{0:T(1024)S(1)} %get-tuple-element.9, ...), kind=kOutput, calls=%fused_computation.20 | convolution fusion | flops 3246915584 | bytes 16797696 | tf_op jit(solution)/shard_map/dot_general | solution.py:27
  366.2 6.1 all-to-all-start
  372.3 34.1 %all-to-all-done = bf16[8,128,512]{2,1,0:T(8,128)(2,1)S(1)} async-done(((bf16[8,128,512]{2,1,0:T(8,128)(2,1)}), bf16[8,128,512]{2,1,0:T(8,128)(2,1)S(1)}, u32[]{:S(2)}, u32[]{:S(2)}) %all-to-all-start) | async-done | bytes 1048608 | tf_op jit(solution)/shard_map/all_to_all | solution.py:32
  406.5 2.3 select_bitcast_fusion.1
  408.8 414.6 %reduce-scatter.4.cloned.1.call-done = f32[8,4096]{1,0:T(8,128)} async-done(((f32[1024,4096]{1,0:T(8,128)}), f32[8,4096]{1,0:T(8,128)}) %reduce-scatter.4.cloned.1.call-update) | async-done | bytes 131088
  823.3 1.5 copy.15
  824.9 1.5 select_bitcast_fusion
  826.4 2.8 copy.13
  (23 shorter events, 0.8 us)
Async XLA Ops:
  8.0 108.3 %copy-start = (bf16[128,1024]{1,0:T(8,128)(2,1)S(1)}, bf16[128,1024]{1,0:T(8,128)(2,1)}, u32[]{:S(2)}) copy-start(bf16[128,1024]{1,0:T(8,128)(2,1)} %param.14) | copy-start | bytes 786436
  8.0 63.5 %all-gather.6.cloned.1.call-start = ((), (), s32[]{:S(2)}) async-start(), calls=%async_computation.3 | async-start | bytes 10027008 | tf_op jit(solution)/shard_map/all_gather | solution.py:17
  8.7 140.0 %all-gather.4.cloned.1.call-start = ((), (), s32[]{:S(2)}) async-start(), calls=%async_computation.2 | async-start | bytes 7077888 | tf_op jit(solution)/shard_map/all_gather | solution.py:22
  9.5 305.4 %all-reduce.2.cloned.1.call-start = ((), (), s32[]{:S(2)}) async-start(), calls=%async_computation.4 | async-start | bytes 12582912 | tf_op jit(solution)/shard_map/psum | solution.py:21
  86.7 1.2 copy-start.2
  86.7 6.3 copy-start.4
  86.7 269.4 %all-gather.8.cloned.1.call-start = ((), (), s32[]{:S(2)}) async-start(), calls=%async_computation.5 | async-start | bytes 3342336 | tf_op jit(solution)/shard_map/all_gather | solution.py:29
  87.3 736.0 %reduce-scatter.4.cloned.1.call-start = ((), (), s32[]{:S(2)}) async-start(), calls=%async_computation.6 | async-start | bytes 16908288
  87.9 27.6 %collective-permute-start = (bf16[128,4096]{1,0:T(8,128)(2,1)S(1)}, bf16[128,4096]{1,0:T(8,128)(2,1)S(1)}, u32[]{:S(2)}, u32[]{:S(2)}) collective-permute-start(bf16[128,4096]{1,0:T(8,128)(2,1)S(1)} %bitcast.20), channel_id=1, source_target_pairs={{0,128},{1,129},{2,130},{3,131},{4,132},{5,133},{6,134},{7,135},{8... | collective-permute-start | bytes 3145736 | tf_op jit(solution)/shard_map/ppermute | solution.py:10
  142.5 213.7 %copy-start.3 = (f32[3072]{0:T(1024)S(1)}, f32[3072]{0:T(1024)}, u32[]{:S(2)}) copy-start(f32[3072]{0:T(1024)} %param.12) | copy-start | bytes 36868
  366.2 40.2 %all-to-all-start = ((bf16[8,128,512]{2,1,0:T(8,128)(2,1)}), bf16[8,128,512]{2,1,0:T(8,128)(2,1)S(1)}, u32[]{:S(2)}, u32[]{:S(2)}) async-start(bf16[8,128,512]{2,1,0:T(8,128)(2,1)} %bitcast.23), calls=%async_computation | async-start | bytes 2097152 | tf_op jit(solution)/shard_map/all_to_all | solution.py:32
  823.3 5.9 copy-start.1
Sparse Core Ops, SparseCore 0:
  10.7 60.8 all-gather.5
  73.4 75.3 all-gather.3
  151.2 163.6 all-reduce.1
  316.6 39.5 all-gather.7
Sparse Core Ops, SparseCore 1:
  142.5 680.7 reduce-scatter.3
where the time goes:
time: 837 us; the launch traced here: 836 us
  waiting for transfers between devices  741 us (89%)
  matrix products  33.7 us (4%)
  local copies, waits for them, and re-layouts  22.6 us (3%)
  between operations  15.3 us (2%)
  other arithmetic  11.9 us (1%)
  starting transfers between devices  11.3 us (1%)
    unnamed x6, waiting for transfers between devices  417 us
    psum x1, waiting for transfers between devices, teacher_work(): lax.psum(partial_sum.astype(jnp.bfloat16), 'mp').astype(jnp.float32)  166 us
    all_gather x1, waiting for transfers between devices, teacher_work(): lax.all_gather(w_down, 'dp', axis=0, tiled=True)  62 us
    all_gather x1, waiting for transfers between devices, teacher_work(): lax.all_gather(head_weight, 'dp', axis=0, tiled=True)  34.6 us
    all_to_all x1, waiting for transfers between devices, teacher_work(): lax.all_to_all(logits.astype(jnp.bfloat16), 'mp', split_axis=0, concat_ax...  34.1 us
    unnamed x13, local copies, waits for them, and re-layouts  22.5 us
    ppermute x1, waiting for transfers between devices, passed_along(): return lax.ppermute(block, axis, route)  21.8 us
  transfers between devices with their start and end apart: 7, of which 7 were waited for; matrix products, arithmetic and copies ran while one was open for 7% of the time, Pallas kernels for 0%

commit v1 on v0

v1 whole, which is shorter than its diff:
```python
import jax
import jax.numpy as jnp
from jax import lax
from jax.experimental import pallas as pl
from jax.experimental.pallas import tpu as pltpu
from jax.sharding import Mesh, PartitionSpec as P

F32 = jnp.float32
BF16 = jnp.bfloat16
N_MP = 8
DP = ("yl", "x", "core")


def ring(n, k):
    return [(i, (i + k) % n) for i in range(n)]


def z_up(a):
    return lax.ppermute(a, "mp", ring(N_MP, 1))


def z_down(a):
    return lax.ppermute(a, "mp", ring(N_MP, -1))


def swap(a, axis):
    return lax.ppermute(a, axis, ring(2, 1))


def plus(a, b):
    return (a.astype(F32) + b.astype(F32)).astype(a.dtype)


def scatter_sum_z(part):
    half = part[4].shape[0] // 2
    r = z_up(part[4][:half])
    l = z_down(part[4][half:])
    a, b = part[3], part[5]
    r = z_up(jnp.concatenate([plus(a[:half], r), a[half:]], axis=0))
    l = z_down(jnp.concatenate([b[:half], plus(b[half:], l)], axis=0))
    r = z_up(plus(part[2], r))
    l = z_down(plus(part[6], l))
    passed = r
    r = z_up(plus(part[1], r))
    l = z_down(plus(part[7], l))
    return part[0].astype(F32) + r.astype(F32) + l.astype(F32), passed


def after(value, *earlier):
    ready = True
    for a in earlier:
        ready = ready & (a[(0,) * a.ndim].astype(F32) < 3e38)
    return jnp.where(ready, value, jnp.zeros_like(value))


def norm_kernel(place_ref, a_ref, b_ref, ga_ref, gb_ref, stream_ref, gain_ref, out_ref):
    s = place_ref[0]
    rows = a_ref.shape[1] // 8
    sums = [[], []]
    for own_ref, got_ref in ((a_ref, ga_ref), (b_ref, gb_ref)):
        own, got = own_ref[...].astype(F32), got_ref[...].astype(F32)
        sums[0].append(jnp.where(s == 0, own, got))
        sums[1].append(jnp.where(s == 0, got, own))
    pieces = []
    for d in range(16):
        at = (d % 8) * rows
        for sec in (0, 1):
            pieces.append(sums[sec][d // 8][:, at : at + rows])
    down_sum = jnp.concatenate(pieces, axis=1)
    stream = jnp.concatenate([stream_ref[m] for m in range(N_MP)], axis=1).astype(F32)
    middle = stream + 0.5 * down_sum
    center = jnp.mean(middle, axis=1, keepdims=True)
    spread = jnp.mean(middle * middle, axis=1, keepdims=True) - center * center
    normed = (middle - center) * lax.rsqrt(spread + 1e-05) * gain_ref[...]
    out_ref[...] = normed.astype(BF16)


def normalize(place, sums, got, stream, gain):
    frames = stream.shape[1]
    step = 32
    part = pl.BlockSpec((step, sums[0].shape[1]), lambda i, _: (i, 0))
    return pl.pallas_call(
        norm_kernel,
        grid_spec=pltpu.PrefetchScalarGridSpec(
            num_scalar_prefetch=1,
            grid=(frames // step,),
            in_specs=[
                part,
                part,
                part,
                part,
                pl.BlockSpec((N_MP, step, stream.shape[2]), lambda i, _: (0, i, 0)),
                pl.BlockSpec((1, gain.shape[1]), lambda i, _: (0, 0)),
            ],
            out_specs=pl.BlockSpec((step, gain.shape[1]), lambda i, _: (i, 0)),
        ),
        out_shape=jax.ShapeDtypeStruct((frames, gain.shape[1]), BF16),
        compiler_params=pltpu.CompilerParams(vmem_limit_bytes=24 * 1024 * 1024),
        name="normalize",
    )(place, *sums, *got, stream, gain)


def assemble_kernel(place_ref, logits_ref, far_ref, low_ref, high_ref, out_ref):
    teacher = place_ref[0] == 0
    wide = logits_ref.shape[1] // N_MP
    half = low_ref.shape[0]
    for m in range(N_MP):
        for part, ref in ((0, logits_ref), (1, far_ref)):
            at = pl.ds((2 * m + part) * wide, wide)
            for first, grad_ref in ((0, low_ref), (half, high_ref)):
                rows = pl.ds(first, half)
                out_ref[rows, at] = jnp.where(
                    teacher, ref[rows, pl.ds(m * wide, wide)], grad_ref[:, at]
                )


def assemble(place, logits, far, low, high):
    return pl.pallas_call(
        assemble_kernel,
        in_specs=[pl.BlockSpec(memory_space=pltpu.SMEM)]
        + [pl.BlockSpec(memory_space=pltpu.VMEM)] * 4,
        out_specs=pl.BlockSpec(memory_space=pltpu.VMEM),
        out_shape=jax.ShapeDtypeStruct((logits.shape[0], 2 * logits.shape[1]), BF16),
        compiler_params=pltpu.CompilerParams(vmem_limit_bytes=24 * 1024 * 1024),
        name="assemble",
    )(place.astype(jnp.int32), logits, far, low, high)


def body(
    hidden_pre, residual, w_down, head_weight, norm_gain, segment_logits, student_hidden, frame_mask
):
    s = lax.axis_index("sec")
    z = lax.axis_index("mp")
    frames = student_hidden.shape[0]
    half = frames // 2
    vocab = segment_logits.shape[2]
    rows = w_down.shape[0] // 2

    weights = lax.dynamic_slice_in_dim(w_down, s * rows, rows, 0)
    weights = lax.all_gather(weights, DP, axis=0, tiled=True)

    wide = head_weight.shape[1] // 2
    head = lax.dynamic_slice_in_dim(head_weight, s * wide, wide, 1)
    head = lax.all_to_all(
        jnp.broadcast_to(head[None], (N_MP,) + head.shape), "mp", 0, 0, tiled=True
    )
    head_part = head.transpose(1, 0, 2).reshape(-1, N_MP * wide)
    head = lax.all_gather(head_part, DP, axis=0, tiled=True)

    active = [
        lax.dynamic_slice_in_dim(hidden_pre, ((z + k) % N_MP) * frames, frames, 0)
        for k in range(N_MP)
    ]
    active[0] = after(active[0], head_part)
    active = jax.nn.silu(jnp.concatenate(active, axis=0).astype(F32)).astype(BF16)
    parts = [
        lax.dot_general(
            active, w, (((1,), (1,)), ((), ())), preferred_element_type=F32
        ).astype(BF16)
        for w in jnp.split(weights, 2, axis=0)
    ]
    sums, passed = zip(*[scatter_sum_z(p.reshape(N_MP, frames, -1)) for p in parts])
    sums = [a.astype(BF16) for a in sums]
    got = [swap(a, "sec") for a in sums]
    stream = lax.all_to_all(
        after(residual, head_part).reshape(N_MP, frames, -1), "mp", 0, 0, tiled=True
    )
    normed = normalize(s.reshape(1).astype(jnp.int32), sums, got, stream, norm_gain[None])
    logits = jnp.dot(normed, head, preferred_element_type=F32).astype(BF16)
    far = lax.ppermute(logits, "sec", [(1, 0)])
    own_logits = segment_logits[0]
    sent = lax.dynamic_slice_in_dim(own_logits, (1 - s) * half, half, 0)
    held = lax.dynamic_slice_in_dim(own_logits, s * half, half, 0)
    came = after(swap(sent, "sec"), parts[1])
    p_held = jax.nn.softmax(held.astype(F32), axis=-1)
    p_came = jax.nn.softmax(came.astype(F32), axis=-1)
    mask = lax.dynamic_slice_in_dim(frame_mask, s * half, half, 0).astype(F32)[:, None]
    sign = jnp.where(s == 0, -1.0, 1.0).astype(F32)
    grad = (mask * (sign * (p_held - p_came))).astype(BF16)
    grad_far = lax.ppermute(grad, "sec", [(0, 1)])
    hidden = lax.dynamic_slice_in_dim(student_hidden, s * half, half, 0)
    hidden = lax.all_to_all(
        jnp.broadcast_to(hidden[None], (16,) + hidden.shape), DP, 0, 0, tiled=True
    ).reshape(16 * half, -1)
    cols = vocab // 16
    grad_cols = lax.all_to_all(
        grad.reshape(half, 16, cols).transpose(1, 0, 2), DP, 0, 0, tiled=True
    ).reshape(16 * half, cols)
    grad_cols = after(grad_cols, grad_far, passed[0], passed[1])
    product = lax.dot_general(
        hidden, grad_cols, (((0,), (0,)), ((), ())), preferred_element_type=F32
    )
    units = product.shape[0] // (16 * N_MP)
    product = product.reshape(16, N_MP, units, cols)
    product = [
        lax.dynamic_index_in_dim(product, (z + k) % N_MP, 1, keepdims=False).reshape(-1, cols)
        for k in range(N_MP)
    ]
    share, _ = scatter_sum_z(product)
    share = after(share.reshape(16, units, cols), normed)
    share = share + lax.ppermute(share, "sec", [(0, 1)])
    weight_grad = lax.all_to_all(share, DP, 0, 0, tiled=True)
    weight_grad = weight_grad.transpose(1, 0, 2).reshape(units, vocab)

    is_teacher = s == 0
    segment = assemble(s.reshape(1), logits, far, grad_far, grad)
    return (segment[None], jnp.where(is_teacher, 0.0, weight_grad)[None])


def solution(mesh):
    fine = Mesh(mesh.devices.reshape(2, 2, 4, 2, N_MP), ("sec",) + DP + ("mp",))
    placed = (
        P(DP, "mp"),
        P(DP, "mp"),
        P(DP, "mp"),
        P(DP, "mp"),
        P(),
        P("sec", DP + ("mp",), None),
        P(DP + ("mp",), None),
        P(DP + ("mp",)),
    )
    return jax.shard_map(
        body,
        mesh=fine,
        in_specs=placed,
        out_specs=(P("sec", DP + ("mp",), None), P("sec", DP + ("mp",), None)),
        check_vma=False,
    )
```

time: 837 us -> 237 us (0.28)
  waiting for transfers between devices: 741 us -> 40 us
  starting transfers between devices: 11.3 us -> 68.3 us
  blocking collectives: 0 us -> 41.5 us
  matrix products: 33.7 us -> 20.4 us
    unnamed x6 -> x2, waiting for transfers between devices: 417 us -> 0.03 us
    psum x1 -> x0, waiting for transfers between devices: 166 us -> none  [teacher_work(): lax.psum(partial_sum.astype(jnp.bfloat16), 'mp').astype(jnp.float32)]
    all_gather x3 -> x2, waiting for transfers between devices: 103 us -> 0.02 us  [the longest x1 0.02 us: body(): head = lax.all_gather(head_part, DP, axis=0, tiled=True)]
    ppermute x1 -> x30, starting transfers between devices: 5.05 us -> 55.6 us  [the longest x12 29.3 us: z_down(): return lax.ppermute(a, 'mp', ring(N_MP, -1))]
    all_to_all x0 -> x2, blocking collectives: none -> 41.5 us  [the longest x1 29.8 us: body(): lax.all_to_all(jnp.broadcast_to(head[None], (N_MP,) + head.shape), 'mp',...]
    all_to_all x1 -> x3, waiting for transfers between devices: 34.1 us -> 0.01 us  [the longest x1 0.01 us: body(): lax.all_to_all(jnp.broadcast_to(hidden[None], (16,) + hidden.shape), DP,...]
    ppermute x1 -> x30, waiting for transfers between devices: 21.8 us -> 40 us  [the longest x12 24.5 us: z_up(): return lax.ppermute(a, 'mp', ring(N_MP, 1))]
    unnamed x13 -> x38, local copies, waits for them, and re-layouts: 22.5 us -> 8.73 us
  transfers between devices with their start and end apart: 7 -> 35, of which waited for: 7 -> 10; matrix products, arithmetic and copies ran while one was open for 7% -> 26% of each run, Pallas kernels for 0% -> 1%
where the time goes in v1:
time: 237 us; the launch traced here: 232 us
  starting transfers between devices  68.3 us (29%)
  blocking collectives  41.5 us (18%)
  waiting for transfers between devices  40 us (17%)
  local copies, waits for them, and re-layouts  23.5 us (10%)
  matrix products  20.4 us (9%)
  between operations  18.7 us (8%)
  other arithmetic  17.2 us (7%)
  Pallas kernels  2.57 us (1%)
    all_to_all x1, blocking collectives, body(): lax.all_to_all(jnp.broadcast_to(head[None], (N_MP,) + head.shape), 'mp',...  29.8 us
    ppermute x12, starting transfers between devices, z_down(): return lax.ppermute(a, 'mp', ring(N_MP, -1))  29.3 us
    ppermute x12, waiting for transfers between devices, z_up(): return lax.ppermute(a, 'mp', ring(N_MP, 1))  24.5 us
    all_to_all x1, blocking collectives, body(): weight_grad = lax.all_to_all(share, DP, 0, 0, tiled=True)  11.8 us
    dot_general x2, matrix products, body(): lax.dot_general(active, w, (((1,), (1,)), ((), ())), preferred_element_ty...  11.6 us
    ppermute x3, waiting for transfers between devices, swap(): return lax.ppermute(a, axis, ring(2, 1))  11.5 us
    ppermute x12, starting transfers between devices, z_up(): return lax.ppermute(a, 'mp', ring(N_MP, 1))  9.29 us
    unnamed x38, local copies, waits for them, and re-layouts  8.73 us
  transfers between devices with their start and end apart: 35, of which 10 were waited for; matrix products, arithmetic and copies ran while one was open for 26% of the time, Pallas kernels for 1%

profile of v1, /device:TPU:0, one launch (start us, length us, event | category | flops | bytes accessed | tf_op | source)
XLA Modules:
  0.0 232.3 jit_solution(14631424501576057969)
XLA Ops:
  10.0 29.8 %all_to_all.25 = bf16[8,192,256]{2,1,0:T(8,128)(2,1)S(1)} all-to-all(bf16[8,192,256]{2,1,0:T(8,128)(2,1)S(1)} %broadcast_in_dim.22), channel_id=1, replica_groups=mesh['sec'=2,'yl'=2,'x'=4,'core'=2,'mp'=8] {'mp'}, dimensions={0} | all-to-all | bytes 1572864 | tf_op jit(solution)/shard_map/all_to_all | solution.py:144
  41.0 3.3 %collective-permute-start.19 = (bf16[64,4096]{1,0:T(8,128)(2,1)S(1)}, bf16[64,4096]{1,0:T(8,128)(2,1)S(1)}, u32[]{:S(2)}, u32[]{:S(2)}) collective-permute-start(bf16[64,4096]{1,0:T(8,128)(2,1)S(1)} %get-tuple-element.27), channel_id=1, source_target_pairs={{0,128},{128,0},{1,129},{129,1},{2,130},{130,2},{3,131},{131,3},{4... | collective-permute-start | bytes 1572872 | tf_op jit(solution)/shard_map/ppermute | solution.py:27
  46.0 4.6 %all-to-all-start.2 = ((bf16[16,64,1024]{2,1,0:T(8,128)(2,1)}), bf16[16,64,1024]{2,1,0:T(8,128)(2,1)}, u32[]{:S(2)}, u32[]{:S(2)}) async-start(bf16[16,64,1024]{2,1,0:T(8,128)(2,1)} %broadcast_in_dim.50), calls=%async_computation.2 | async-start | bytes 4194304 | tf_op jit(solution)/shard_map/all_to_all | solution.py:182
  63.6 6.2 %fusion.11 = bf16[1024,768]{1,0:T(8,128)(2,1)S(1)} fusion(bf16[1536,1536]{1,0:T(8,128)(2,1)} %all-gather.3.cloned.1.call-done, bf16[1024,1536]{1,0:T(8,128)(2,1)} %dynamic-slice_dynamic-update-slice_fusion), kind=kOutput, calls=%fused_computation.12 | convolution fusion | flops 2426142720 | bytes 7077888 | tf_op jit(solution)/shard_map/dot_general | solution.py:157
  71.1 8.7 %collective-permute-done.19 = bf16[64,4096]{1,0:T(8,128)(2,1)S(1)} collective-permute-done((bf16[64,4096]{1,0:T(8,128)(2,1)S(1)}, bf16[64,4096]{1,0:T(8,128)(2,1)S(1)}, u32[]{:S(2)}, u32[]{:S(2)}) %collective-permute-start.19) | collective-permute-done | bytes 524320 | tf_op jit(solution)/shard_map/ppermute | solution.py:27
  80.0 5.4 %fusion.8 = bf16[1024,768]{1,0:T(8,128)(2,1)S(1)} fusion(bf16[1536,1536]{1,0:T(8,128)(2,1)S(1)} %copy-done.14, bf16[1024,1536]{1,0:T(8,128)(2,1)} %dynamic-slice_dynamic-update-slice_fusion), kind=kOutput, calls=%fused_computation.11 | convolution fusion | flops 2426142720 | bytes 7077888 | tf_op jit(solution)/shard_map/dot_general | solution.py:157
  87.2 7.8 %collective-permute-start.4 = (bf16[64,768]{1,0:T(8,128)(2,1)S(1)}, bf16[64,768]{1,0:T(8,128)(2,1)S(1)}, u32[]{:S(2)}, u32[]{:S(2)}) collective-permute-start(bf16[64,768]{1,0:T(8,128)(2,1)S(1)} %get-tuple-element.15), channel_id=1, source_target_pairs={{0,7},{1,0},{2,1},{3,2},{4,3},{5,4},{6,5},{7,6},{8,15},{9,8},{10,9... | collective-permute-start | bytes 294920 | tf_op jit(solution)/shard_map/ppermute | solution.py:23
  96.0 5.4 %collective-permute-start.20 = (bf16[64,4096]{1,0:T(8,128)(2,1)S(1)}, bf16[64,4096]{1,0:T(8,128)(2,1)S(1)}, u32[]{:S(2)}, u32[]{:S(2)}) collective-permute-start(bf16[64,4096]{1,0:T(8,128)(2,1)S(1)} %fusion.21.high_ref), channel_id=1, source_target_pairs={{0,128},{1,129},{2,130},{3,131},{4,132},{5,133},{6,134},{7,135},{8... | collective-permute-start | bytes 1572872 | tf_op jit(solution)/shard_map/ppermute | solution.py:180
  106.1 4.2 %collective-permute-done.8 = bf16[64,768]{1,0:T(8,128)(2,1)S(1)} collective-permute-done((bf16[64,768]{1,0:T(8,128)(2,1)S(1)}, bf16[64,768]{1,0:T(8,128)(2,1)S(1)}, u32[]{:S(2)}, u32[]{:S(2)}) %collective-permute-start.8) | collective-permute-done | bytes 98336 | tf_op jit(solution)/shard_map/ppermute | solution.py:19
  111.1 3.2 %collective-permute-start.13 = (bf16[128,768]{1,0:T(8,128)(2,1)}, bf16[128,768]{1,0:T(8,128)(2,1)}, u32[]{:S(2)}, u32[]{:S(2)}) collective-permute-start(bf16[128,768]{1,0:T(8,128)(2,1)} %pad_maximum_fusion.3), channel_id=1, source_target_pairs={{0,7},{1,0},{2,1},{3,2},{4,3},{5,4},{6,5},{7,6},{8,15},{9,8},{10,9... | collective-permute-start | bytes 589832 | tf_op jit(solution)/shard_map/ppermute | solution.py:23
  115.0 3.7 %collective-permute-done.9 = bf16[128,768]{1,0:T(8,128)(2,1)S(1)} collective-permute-done((bf16[128,768]{1,0:T(8,128)(2,1)S(1)}, bf16[128,768]{1,0:T(8,128)(2,1)S(1)}, u32[]{:S(2)}, u32[]{:S(2)}) %collective-permute-start.9) | collective-permute-done | bytes 196640 | tf_op jit(solution)/shard_map/ppermute | solution.py:19
  119.5 3.6 %all-to-all-start.3 = ((bf16[16,64,256]{2,1,0:T(8,128)(2,1)}), bf16[16,64,256]{2,1,0:T(8,128)(2,1)S(1)}, u32[]{:S(2)}, u32[]{:S(2)}) async-start(bf16[16,64,256]{2,1,0:T(8,128)(2,1)} %bitcast.77), calls=%async_computation.3 | async-start | bytes 1048576 | tf_op jit(solution)/shard_map/all_to_all | solution.py:186
  124.1 3.9 %copy.15 = bf16[1024,1024]{1,0:T(8,128)(2,1)} copy(bf16[1024,1024]{0,1:T(8,128)(2,1)} %bitcast.11) | data formatting | bytes 4194304 | tf_op jit(solution)/shard_map/dot_general | solution.py:190
  128.7 3.2 %collective-permute-start.5 = (bf16[128,768]{1,0:T(8,128)(2,1)}, bf16[128,768]{1,0:T(8,128)(2,1)}, u32[]{:S(2)}, u32[]{:S(2)}) collective-permute-start(bf16[128,768]{1,0:T(8,128)(2,1)} %pad_maximum_fusion.1), channel_id=1, source_target_pairs={{0,7},{1,0},{2,1},{3,2},{4,3},{5,4},{6,5},{7,6},{8,15},{9,8},{10,9... | collective-permute-start | bytes 589832 | tf_op jit(solution)/shard_map/ppermute | solution.py:23
  140.3 4.5 %all-to-all-start.1 = ((bf16[8,128,384]{2,1,0:T(8,128)(2,1)}), bf16[8,128,384]{2,1,0:T(8,128)(2,1)S(1)}, u32[]{:S(2)}, u32[]{:S(2)}) async-start(bf16[8,128,384]{2,1,0:T(8,128)(2,1)} %bitcast.3), calls=%async_computation.1 | async-start | bytes 1572864 | tf_op jit(solution)/shard_map/all_to_all | solution.py:165
  144.9 2.4 %fusion.32 = f32[16,8,8,256]{3,2,1,0:T(8,128)S(1)} fusion(bf16[16,8,8,1024]{3,2,1,0:T(8,128)(2,1)} %bitcast.80, bf16[1024,256,1,1]{1,0,3,2:T(8,128)(2,1)S(1)} %bitcast.84), kind=kOutput, calls=%fused_computation.81 | convolution fusion | flops 536870912 | bytes 3670016 | tf_op jit(solution)/shard_map/dot_general | solution.py:190
  153.8 9.9 %collective-permute-done.21 = f32[64,256]{1,0:T(8,128)S(1)} collective-permute-done((f32[64,256]{1,0:T(8,128)S(1)}, f32[64,256]{1,0:T(8,128)S(1)}, u32[]{:S(2)}, u32[]{:S(2)}) %collective-permute-start.21) | collective-permute-done | bytes 65568 | tf_op jit(solution)/shard_map/ppermute | solution.py:19
  170.4 3.9 %collective-permute-done.22 = f32[128,256]{1,0:T(8,128)S(1)} collective-permute-done((f32[128,256]{1,0:T(8,128)S(1)}, f32[128,256]{1,0:T(8,128)S(1)}, u32[]{:S(2)}, u32[]{:S(2)}) %collective-permute-start.22) | collective-permute-done | bytes 131104 | tf_op jit(solution)/shard_map/ppermute | solution.py:19
  176.5 3.1 %collective-permute-start.7 = (bf16[128,768]{1,0:T(8,128)(2,1)S(1)}, bf16[128,768]{1,0:T(8,128)(2,1)S(1)}, u32[]{:S(2)}, u32[]{:S(2)}) collective-permute-start(bf16[128,768]{1,0:T(8,128)(2,1)S(1)} %add_convert_fusion.6), channel_id=1, source_target_pairs={{0,7},{1,0},{2,1},{3,2},{4,3},{5,4},{6,5},{7,6},{8,15},{9,8},{10,9... | collective-permute-start | bytes 589832 | tf_op jit(solution)/shard_map/ppermute | solution.py:23
  179.7 2.8 %collective-permute-done.23 = f32[128,256]{1,0:T(8,128)S(1)} collective-permute-done((f32[128,256]{1,0:T(8,128)S(1)}, f32[128,256]{1,0:T(8,128)S(1)}, u32[]{:S(2)}, u32[]{:S(2)}) %collective-permute-start.23) | collective-permute-done | bytes 131104 | tf_op jit(solution)/shard_map/ppermute | solution.py:19
  186.5 3.6 %collective-permute-start.16 = (bf16[128,768]{1,0:T(8,128)(2,1)S(1)}, bf16[128,768]{1,0:T(8,128)(2,1)S(1)}, u32[]{:S(2)}, u32[]{:S(2)}) collective-permute-start(bf16[128,768]{1,0:T(8,128)(2,1)S(1)} %add_convert_fusion.5.a_ref), channel_id=1, source_target_pairs={{0,128},{128,0},{1,129},{129,1},{2,130},{130,2},{3,131},{131,3},{4... | collective-permute-start | bytes 589832 | tf_op jit(solution)/shard_map/ppermute | solution.py:27
  199.7 3.4 %collective-permute-start.29 = (f32[16,8,256]{2,1,0:T(8,128)S(1)}, f32[16,8,256]{2,1,0:T(8,128)S(1)}, u32[]{:S(2)}, u32[]{:S(2)}) collective-permute-start(f32[16,8,256]{2,1,0:T(8,128)S(1)} %fusion.25), channel_id=1, source_target_pairs={{0,128},{1,129},{2,130},{3,131},{4,132},{5,133},{6,134},{7,135},{8... | collective-permute-start | bytes 393224 | tf_op jit(solution)/shard_map/ppermute | solution.py:201
  203.1 6.4 %convolution_convert_fusion.logits_ref = bf16[128,2048]{1,0:T(8,128)(2,1)S(1)} fusion(bf16[128,3072]{1,0:T(8,128)(2,1)S(1)} %normalize.1, bf16[3072,2048]{1,0:T(8,128)(2,1)} %all-gather.5.cloned.1.call-done), kind=kOutput, calls=%fused_computation.6 | convolution fusion | flops 1610874880 | bytes 13893632 | tf_op jit(solution)/shard_map/dot_general | solution.py:169
  211.9 11.8 %all_to_all.26 = f32[16,8,256]{2,1,0:T(8,128)S(1)} all-to-all(f32[16,8,256]{2,1,0:T(8,128)S(1)} %fusion.37), channel_id=1, replica_groups=mesh['sec'=2,'yl'=2,'x'=4,'core'=2,'mp'=8] {'yl','x','core'}, dimensions={0} | all-to-all | bytes 262144 | tf_op jit(solution)/shard_map/all_to_all | solution.py:202
  (146 shorter events, 68.8 us)
Async XLA Ops:
  7.2 56.4 %all-gather.3.cloned.1.call-start = ((), (), s32[]{:S(2)}) async-start(), calls=%async_computation.5 | async-start | bytes 5013504 | tf_op jit(solution)/shard_map/all_gather | solution.py:140
  9.0 194.1 %all-gather.5.cloned.1.call-start = ((), (), s32[]{:S(2)}) async-start(), calls=%async_computation.6 | async-start | bytes 13369344 | tf_op jit(solution)/shard_map/all_gather | solution.py:148
  41.0 38.8 %collective-permute-start.19 = (bf16[64,4096]{1,0:T(8,128)(2,1)S(1)}, bf16[64,4096]{1,0:T(8,128)(2,1)S(1)}, u32[]{:S(2)}, u32[]{:S(2)}) collective-permute-start(bf16[64,4096]{1,0:T(8,128)(2,1)S(1)} %get-tuple-element.27), channel_id=1, source_target_pairs={{0,128},{128,0},{1,129},{129,1},{2,130},{130,2},{3,131},{131,3},{4... | collective-permute-start | bytes 1572872 | tf_op jit(solution)/shard_map/ppermute | solution.py:27
  46.0 73.5 %all-to-all-start.2 = ((bf16[16,64,1024]{2,1,0:T(8,128)(2,1)}), bf16[16,64,1024]{2,1,0:T(8,128)(2,1)}, u32[]{:S(2)}, u32[]{:S(2)}) async-start(bf16[16,64,1024]{2,1,0:T(8,128)(2,1)} %broadcast_in_dim.50), calls=%async_computation.2 | async-start | bytes 4194304 | tf_op jit(solution)/shard_map/all_to_all | solution.py:182
  85.4 18.9 %collective-permute-start = (bf16[64,768]{1,0:T(8,128)(2,1)S(1)}, bf16[64,768]{1,0:T(8,128)(2,1)S(1)}, u32[]{:S(2)}, u32[]{:S(2)}) collective-permute-start(bf16[64,768]{1,0:T(8,128)(2,1)S(1)} %get-tuple-element.14), channel_id=1, source_target_pairs={{0,1},{1,2},{2,3},{3,4},{4,5},{5,6},{6,7},{7,0},{8,9},{9,10},{10,1... | collective-permute-start | bytes 294920 | tf_op jit(solution)/shard_map/ppermute | solution.py:19
  87.2 17.1 %collective-permute-start.4 = (bf16[64,768]{1,0:T(8,128)(2,1)S(1)}, bf16[64,768]{1,0:T(8,128)(2,1)S(1)}, u32[]{:S(2)}, u32[]{:S(2)}) collective-permute-start(bf16[64,768]{1,0:T(8,128)(2,1)S(1)} %get-tuple-element.15), channel_id=1, source_target_pairs={{0,7},{1,0},{2,1},{3,2},{4,3},{5,4},{6,5},{7,6},{8,15},{9,8},{10,9... | collective-permute-start | bytes 294920 | tf_op jit(solution)/shard_map/ppermute | solution.py:23
  96.0 43.1 %collective-permute-start.20 = (bf16[64,4096]{1,0:T(8,128)(2,1)S(1)}, bf16[64,4096]{1,0:T(8,128)(2,1)S(1)}, u32[]{:S(2)}, u32[]{:S(2)}) collective-permute-start(bf16[64,4096]{1,0:T(8,128)(2,1)S(1)} %fusion.21.high_ref), channel_id=1, source_target_pairs={{0,128},{1,129},{2,130},{3,131},{4,132},{5,133},{6,134},{7,135},{8... | collective-permute-start | bytes 1572872 | tf_op jit(solution)/shard_map/ppermute | solution.py:180
  104.4 9.9 %collective-permute-start.1 = (bf16[128,768]{1,0:T(8,128)(2,1)S(1)}, bf16[128,768]{1,0:T(8,128)(2,1)S(1)}, u32[]{:S(2)}, u32[]{:S(2)}) collective-permute-start(bf16[128,768]{1,0:T(8,128)(2,1)S(1)} %pad_maximum_fusion), channel_id=1, source_target_pairs={{0,1},{1,2},{2,3},{3,4},{4,5},{5,6},{6,7},{7,0},{8,9},{9,10},{10,1... | collective-permute-start | bytes 589832 | tf_op jit(solution)/shard_map/ppermute | solution.py:19
  111.1 24.0 %collective-permute-start.13 = (bf16[128,768]{1,0:T(8,128)(2,1)}, bf16[128,768]{1,0:T(8,128)(2,1)}, u32[]{:S(2)}, u32[]{:S(2)}) collective-permute-start(bf16[128,768]{1,0:T(8,128)(2,1)} %pad_maximum_fusion.3), channel_id=1, source_target_pairs={{0,7},{1,0},{2,1},{3,2},{4,3},{5,4},{6,5},{7,6},{8,15},{9,8},{10,9... | collective-permute-start | bytes 589832 | tf_op jit(solution)/shard_map/ppermute | solution.py:23
  115.0 16.9 %collective-permute-start.2 = (bf16[128,768]{1,0:T(8,128)(2,1)}, bf16[128,768]{1,0:T(8,128)(2,1)S(1)}, u32[]{:S(2)}, u32[]{:S(2)}) collective-permute-start(bf16[128,768]{1,0:T(8,128)(2,1)} %add_convert_fusion.9), channel_id=1, source_target_pairs={{0,1},{1,2},{2,3},{3,4},{4,5},{5,6},{6,7},{7,0},{8,9},{9,10},{10,1... | collective-permute-start | bytes 589832 | tf_op jit(solution)/shard_map/ppermute | solution.py:19
  119.5 13.7 %collective-permute-start.10 = (bf16[128,768]{1,0:T(8,128)(2,1)}, bf16[128,768]{1,0:T(8,128)(2,1)}, u32[]{:S(2)}, u32[]{:S(2)}) collective-permute-start(bf16[128,768]{1,0:T(8,128)(2,1)} %add_convert_fusion.4), channel_id=1, source_target_pairs={{0,1},{1,2},{2,3},{3,4},{4,5},{5,6},{6,7},{7,0},{8,9},{9,10},{10,1... | collective-permute-start | bytes 589832 | tf_op jit(solution)/shard_map/ppermute | solution.py:19
  119.5 20.8 %all-to-all-start.3 = ((bf16[16,64,256]{2,1,0:T(8,128)(2,1)}), bf16[16,64,256]{2,1,0:T(8,128)(2,1)S(1)}, u32[]{:S(2)}, u32[]{:S(2)}) async-start(bf16[16,64,256]{2,1,0:T(8,128)(2,1)} %bitcast.77), calls=%async_computation.3 | async-start | bytes 1048576 | tf_op jit(solution)/shard_map/all_to_all | solution.py:186
  128.7 22.0 %collective-permute-start.5 = (bf16[128,768]{1,0:T(8,128)(2,1)}, bf16[128,768]{1,0:T(8,128)(2,1)}, u32[]{:S(2)}, u32[]{:S(2)}) collective-permute-start(bf16[128,768]{1,0:T(8,128)(2,1)} %pad_maximum_fusion.1), channel_id=1, source_target_pairs={{0,7},{1,0},{2,1},{3,2},{4,3},{5,4},{6,5},{7,6},{8,15},{9,8},{10,9... | collective-permute-start | bytes 589832 | tf_op jit(solution)/shard_map/ppermute | solution.py:23
  137.1 31.0 %collective-permute-start.14 = (bf16[128,768]{1,0:T(8,128)(2,1)}, bf16[128,768]{1,0:T(8,128)(2,1)}, u32[]{:S(2)}, u32[]{:S(2)}) collective-permute-start(bf16[128,768]{1,0:T(8,128)(2,1)} %get-tuple-element.3), channel_id=1, source_target_pairs={{0,7},{1,0},{2,1},{3,2},{4,3},{5,4},{6,5},{7,6},{8,15},{9,8},{10,9... | collective-permute-start | bytes 589832 | tf_op jit(solution)/shard_map/ppermute | solution.py:23
  137.1 47.3 %collective-permute-start.11 = (bf16[128,768]{1,0:T(8,128)(2,1)S(1)}, bf16[128,768]{1,0:T(8,128)(2,1)}, u32[]{:S(2)}, u32[]{:S(2)}) collective-permute-start(bf16[128,768]{1,0:T(8,128)(2,1)S(1)} %get-tuple-element.2), channel_id=1, source_target_pairs={{0,1},{1,2},{2,3},{3,4},{4,5},{5,6},{6,7},{7,0},{8,9},{9,10},{10,1... | collective-permute-start | bytes 589832 | tf_op jit(solution)/shard_map/ppermute | solution.py:19
  140.3 52.9 %all-to-all-start.1 = ((bf16[8,128,384]{2,1,0:T(8,128)(2,1)}), bf16[8,128,384]{2,1,0:T(8,128)(2,1)S(1)}, u32[]{:S(2)}, u32[]{:S(2)}) async-start(bf16[8,128,384]{2,1,0:T(8,128)(2,1)} %bitcast.3), calls=%async_computation.1 | async-start | bytes 1572864 | tf_op jit(solution)/shard_map/all_to_all | solution.py:165
  147.3 16.3 %collective-permute-start.21 = (f32[64,256]{1,0:T(8,128)S(1)}, f32[64,256]{1,0:T(8,128)S(1)}, u32[]{:S(2)}, u32[]{:S(2)}) collective-permute-start(f32[64,256]{1,0:T(8,128)S(1)} %get-tuple-element.22), channel_id=1, source_target_pairs={{0,1},{1,2},{2,3},{3,4},{4,5},{5,6},{6,7},{7,0},{8,9},{9,10},{10,1... | collective-permute-start | bytes 196616 | tf_op jit(solution)/shard_map/ppermute | solution.py:19
  149.4 17.5 %collective-permute-start.25 = (f32[64,256]{1,0:T(8,128)S(1)}, f32[64,256]{1,0:T(8,128)S(1)}, u32[]{:S(2)}, u32[]{:S(2)}) collective-permute-start(f32[64,256]{1,0:T(8,128)S(1)} %get-tuple-element.24), channel_id=1, source_target_pairs={{0,7},{1,0},{2,1},{3,2},{4,3},{5,4},{6,5},{7,6},{8,15},{9,8},{10,9... | collective-permute-start | bytes 196616 | tf_op jit(solution)/shard_map/ppermute | solution.py:23
  151.8 24.4 %collective-permute-start.6 = (bf16[128,768]{1,0:T(8,128)(2,1)S(1)}, bf16[128,768]{1,0:T(8,128)(2,1)S(1)}, u32[]{:S(2)}, u32[]{:S(2)}) collective-permute-start(bf16[128,768]{1,0:T(8,128)(2,1)S(1)} %get-tuple-element.11), channel_id=1, source_target_pairs={{0,7},{1,0},{2,1},{3,2},{4,3},{5,4},{6,5},{7,6},{8,15},{9,8},{10,9... | collective-permute-start | bytes 589832 | tf_op jit(solution)/shard_map/ppermute | solution.py:23
  163.7 22.8 %collective-permute-start.3 = (bf16[128,768]{1,0:T(8,128)(2,1)S(1)}, bf16[128,768]{1,0:T(8,128)(2,1)S(1)}, u32[]{:S(2)}, u32[]{:S(2)}) collective-permute-start(bf16[128,768]{1,0:T(8,128)(2,1)S(1)} %get-tuple-element.10), channel_id=1, source_target_pairs={{0,1},{1,2},{2,3},{3,4},{4,5},{5,6},{6,7},{7,0},{8,9},{9,10},{10,1... | collective-permute-start | bytes 589832 | tf_op jit(solution)/shard_map/ppermute | solution.py:19
  174.3 10.9 %collective-permute-start.15 = (bf16[128,768]{1,0:T(8,128)(2,1)S(1)}, bf16[128,768]{1,0:T(8,128)(2,1)S(1)}, u32[]{:S(2)}, u32[]{:S(2)}) collective-permute-start(bf16[128,768]{1,0:T(8,128)(2,1)S(1)} %add_convert_fusion.1), channel_id=1, source_target_pairs={{0,7},{1,0},{2,1},{3,2},{4,3},{5,4},{6,5},{7,6},{8,15},{9,8},{10,9... | collective-permute-start | bytes 589832 | tf_op jit(solution)/shard_map/ppermute | solution.py:23
  184.4 14.2 %collective-permute-start.24 = (f32[128,256]{1,0:T(8,128)}, f32[128,256]{1,0:T(8,128)}, u32[]{:S(2)}, u32[]{:S(2)}) collective-permute-start(f32[128,256]{1,0:T(8,128)} %get-tuple-element.18), channel_id=1, source_target_pairs={{0,1},{1,2},{2,3},{3,4},{4,5},{5,6},{6,7},{7,0},{8,9},{9,10},{10,1... | collective-permute-start | bytes 393224 | tf_op jit(solution)/shard_map/ppermute | solution.py:19
  199.7 11.1 %collective-permute-start.29 = (f32[16,8,256]{2,1,0:T(8,128)S(1)}, f32[16,8,256]{2,1,0:T(8,128)S(1)}, u32[]{:S(2)}, u32[]{:S(2)}) collective-permute-start(f32[16,8,256]{2,1,0:T(8,128)S(1)} %fusion.25), channel_id=1, source_target_pairs={{0,128},{1,129},{2,130},{3,131},{4,132},{5,133},{6,134},{7,135},{8... | collective-permute-start | bytes 393224 | tf_op jit(solution)/shard_map/ppermute | solution.py:201
  209.5 14.8 %collective-permute-start.18 = (bf16[128,2048]{1,0:T(8,128)(2,1)S(1)}, bf16[128,2048]{1,0:T(8,128)(2,1)S(1)}, u32[]{:S(2)}, u32[]{:S(2)}) collective-permute-start(bf16[128,2048]{1,0:T(8,128)(2,1)S(1)} %convolution_convert_fusion.logits_ref), channel_id=1, source_target_pairs={{128,0},{129,1},{130,2},{131,3},{132,4},{133,5},{134,6},{135,7},{1... | collective-permute-start | bytes 1572872 | tf_op jit(solution)/shard_map/ppermute | solution.py:170
  (27 other events, 427.5 us)
Sparse Core Ops, SparseCore 0:
  10.4 46.4 all-gather.2
  58.8 111.5 all-gather.4
